TPU v7x, 32 devices: a whole 2x2x4 slice. The times are simulated.
32 devices in a mesh: outer: 8 (over y, x, core), inner: 4 (over z).
Axes of the slice: x: 2, y: 2, z: 4, core: 2. Of those that a mesh axis runs over, the one named last changes fastest.
Arguments:
- queries: bfloat16 [8192, 1536], P(('outer', 'inner')), may hold values from -6 to 6
- key_rows: bfloat16 [8192, 1536], P(('outer', 'inner')), may hold values from -6 to 6
- values: bfloat16 [8192, 1536], P(('outer', 'inner')), may hold values from -6 to 6
- out_grads: bfloat16 [8192, 1536], P(('outer', 'inner')), may hold values from -96 to 96
- offsets: int32 [8], replicated, may hold values from 0 to 127, as said below
Outputs:
- grad_queries: bfloat16 [8192, 1536], P(('outer', 'inner'))
- grad_keys: bfloat16 [8192, 1536], P(('outer', 'inner'))
- grad_values: bfloat16 [8192, 1536], P(('outer', 'inner'))
Inputs may be any that keep to these rules, and one draw needn't show every extreme that they name: offsets[j] is below 4 for j < 5 and below 128 for the others.
All inputs are finite; a program needn't handle non-finite values.
Results may differ from a plain program's by a relative error of at most 0.0057.
The roundings to bfloat16 on the way count: a program that leaves them out, or rounds other values in their place, can miss the bound.
Values may be sent and summed in bfloat16 or wider, within the bound.
A program may use at most 64 MiB of HBM per device.

v0:
```python
import math

import jax
import jax.numpy as jnp
from jax import lax
from jax.sharding import PartitionSpec as P

HEAD_DIM = 128
H_NEAR = 4
H_MID = 5
R_MID = 4
R_WIDE = 128


def select_rows(block, head_offsets, stride):
    row_number, columns = block.shape
    head_count = head_offsets.shape[0]
    shaped = block.reshape(row_number // stride, stride, head_count, columns // head_count)
    chosen = jnp.arange(stride, dtype=jnp.int32)[:, None] == head_offsets[None, :]
    masked = jnp.where(chosen[None, :, :, None], shaped, jnp.zeros((), block.dtype))
    return jnp.sum(masked, axis=1)


def spread_rows(picked, head_offsets, stride):
    picked_rows, head_count, head_depth = picked.shape
    chosen = jnp.arange(stride, dtype=jnp.int32)[:, None] == head_offsets[None, :]
    placed = jnp.where(chosen[None, :, :, None], picked[:, None], jnp.zeros((), picked.dtype))
    return placed.reshape(picked_rows * stride, head_count * head_depth)


def score_block(query_row_block, key_tile_block):
    score_scale = 1.0 / math.sqrt(query_row_block.shape[-1])
    return (
        jnp.einsum(
            "agk,igk->gai", query_row_block, key_tile_block, preferred_element_type=jnp.float32
        )
        * score_scale
    )


def score_gradients(weights, product_gradients, row_dots, score_scale):
    weights_bfloat = weights.astype(jnp.bfloat16)
    gradients_bfloat = (weights * (product_gradients - row_dots) * score_scale).astype(jnp.bfloat16)
    return (weights_bfloat, gradients_bfloat)


def rows_with_stats(query_row_block, key_tile_block, value_tile_block, gradient_rows):
    score_scale = 1.0 / math.sqrt(query_row_block.shape[-1])
    logit_scores = score_block(query_row_block, key_tile_block)
    row_max = jnp.max(logit_scores, axis=2, keepdims=True)
    exponent = jnp.exp(logit_scores - row_max)
    row_total = jnp.sum(exponent, axis=2, keepdims=True)
    weights = exponent / row_total
    product_gradients = jnp.einsum(
        "agk,igk->gai", gradient_rows, value_tile_block, preferred_element_type=jnp.float32
    )
    row_dots = jnp.sum(weights * product_gradients, axis=2, keepdims=True)
    weights_bfloat, gradients_bfloat = score_gradients(
        weights, product_gradients, row_dots, score_scale
    )
    return (
        weights_bfloat,
        gradients_bfloat,
        (row_max[:, :, 0], row_total[:, :, 0], row_dots[:, :, 0]),
    )


def whole_rows(query_row_block, key_tile_block, value_tile_block, gradient_rows):
    weights_bfloat, gradients_bfloat, unused = rows_with_stats(
        query_row_block, key_tile_block, value_tile_block, gradient_rows
    )
    return (weights_bfloat, gradients_bfloat)


def query_grad(gradients_bfloat, key_tile_block):
    return jnp.einsum(
        "ywr,ryu->wyu", gradients_bfloat, key_tile_block, preferred_element_type=jnp.float32
    )


def key_grad(gradients_bfloat, query_row_block):
    return jnp.einsum(
        "wfl,fwp->lwp", gradients_bfloat, query_row_block, preferred_element_type=jnp.float32
    )


def body(queries, key_rows, values, out_grads, offsets):
    tokens_here = queries.shape[0]
    near_end = H_NEAR * HEAD_DIM
    mid_end = near_end + H_MID * HEAD_DIM
    mid_offsets = offsets[:H_MID]
    wide_offsets = offsets[H_MID:]
    mid_query = select_rows(queries[:, near_end:mid_end], mid_offsets, R_MID)
    mid_key = select_rows(key_rows[:, near_end:mid_end], mid_offsets, R_MID)
    mid_value = select_rows(values[:, near_end:mid_end], mid_offsets, R_MID)
    mid_grad = select_rows(out_grads[:, near_end:mid_end], mid_offsets, R_MID)
    wide_query = select_rows(queries[:, mid_end:], wide_offsets, R_WIDE)
    wide_key = select_rows(key_rows[:, mid_end:], wide_offsets, R_WIDE)
    wide_value = select_rows(values[:, mid_end:], wide_offsets, R_WIDE)
    wide_grad = select_rows(out_grads[:, mid_end:], wide_offsets, R_WIDE)
    wide_keys_all, wide_values_all = (
        lax.all_gather(wide_key, ("outer", "inner"), axis=0, tiled=True),
        lax.all_gather(wide_value, ("outer", "inner"), axis=0, tiled=True),
    )
    all_keys, all_values = (
        lax.all_gather(mid_key, "inner", axis=0, tiled=True),
        lax.all_gather(mid_value, "inner", axis=0, tiled=True),
    )
    mid_weights, mid_sgrad = whole_rows(mid_query, all_keys, all_values, mid_grad)
    sgrad_part = mid_sgrad
    weight_part = mid_weights
    summed = lax.psum_scatter(
        jnp.stack([key_grad(sgrad_part, mid_query), key_grad(weight_part, mid_grad)], axis=1),
        "inner",
        scatter_dimension=0,
        tiled=True,
    )
    mid_result = [query_grad(mid_sgrad, all_keys), summed[:, 0], summed[:, 1]]
    near_query = queries[:, :near_end].reshape(tokens_here, H_NEAR, HEAD_DIM)
    near_key = key_rows[:, :near_end].reshape(tokens_here, H_NEAR, HEAD_DIM)
    near_value = values[:, :near_end].reshape(tokens_here, H_NEAR, HEAD_DIM)
    near_grad = out_grads[:, :near_end].reshape(tokens_here, H_NEAR, HEAD_DIM)
    near_weights, near_sgrad = whole_rows(near_query, near_key, near_value, near_grad)
    near_result = [
        query_grad(near_sgrad, near_key),
        key_grad(near_sgrad, near_query),
        key_grad(near_weights, near_grad),
    ]
    wide_weights, wide_sgrad = whole_rows(wide_query, wide_keys_all, wide_values_all, wide_grad)
    sgrad_part = wide_sgrad
    weight_part = wide_weights
    wide_summed = lax.psum_scatter(
        jnp.stack([key_grad(sgrad_part, wide_query), key_grad(weight_part, wide_grad)], axis=1),
        ("outer", "inner"),
        scatter_dimension=0,
        tiled=True,
    )
    wide_result = [query_grad(wide_sgrad, wide_keys_all), wide_summed[:, 0], wide_summed[:, 1]]
    joined = []
    for which in range(3):
        near_part = near_result[which].reshape(tokens_here, near_end)
        mid_part = spread_rows(mid_result[which], mid_offsets, R_MID)
        wide_part = spread_rows(wide_result[which], wide_offsets, R_WIDE)
        joined.append(
            jnp.concatenate([near_part, mid_part, wide_part], axis=1).astype(jnp.bfloat16)
        )
    return (joined[0], joined[1], joined[2])


def solution(mesh):
    return jax.shard_map(
        body,
        mesh=mesh,
        in_specs=(
            P(("outer", "inner"), None),
            P(("outer", "inner"), None),
            P(("outer", "inner"), None),
            P(("outer", "inner"), None),
            P(),
        ),
        out_specs=(
            P(("outer", "inner"), None),
            P(("outer", "inner"), None),
            P(("outer", "inner"), None),
        ),
        check_vma=False,
    )
```

profile of v0, /device:TPU:0, one launch (start us, length us, event | category | flops | bytes accessed | tf_op | source)
XLA Modules:
  0.0 287.9 jit_solution(2356767788650697885)
XLA Ops:
  0.6 1.3 dynamic-slice
  4.0 1.0 slice.65
  6.4 2.0 fusion.36
  8.6 70.2 %all_gather.14 = bf16[64,3,128]{2,1,0:T(4,128)(2,1)S(1)} all-gather(bf16[2,3,128]{2,1,0:T(4,128)(2,1)S(1)} %copy.106), channel_id=1, replica_groups=mesh['outer'=8,'inner'=4] {'outer','inner'}, dimensions={0}, use_global_device_ids=true | all-gather | bytes 50688 | tf_op jit(solution)/shard_map/all_gather | solution.py:102
  79.1 63.8 %all_gather.15 = bf16[64,3,128]{2,1,0:T(4,128)(2,1)S(1)} all-gather(bf16[2,3,128]{2,1,0:T(4,128)(2,1)S(1)} %copy.112), channel_id=1, replica_groups=mesh['outer'=8,'inner'=4] {'outer','inner'}, dimensions={0}, use_global_device_ids=true | all-gather | bytes 50688 | tf_op jit(solution)/shard_map/all_gather | solution.py:103
  144.1 42.4 %all-reduce.4 = bf16[64,2,3,128]{3,0,2,1:T(8,128)(2,1)S(1)} all-reduce(f32[64,2,3,128]{3,0,2,1:T(8,128)S(1)} %pad_maximum_fusion.4), channel_id=3, replica_groups=mesh['outer'=8,'inner'=4] {'outer','inner'}, use_global_device_ids=true, to_apply=%region_18.19.clone | all-reduce | flops 49152 | bytes 294912
  187.2 0.8 copy.150
  188.0 0.8 copy.149
  189.1 1.5 select_convert_fusion.3
  190.7 0.8 copy.135
  194.1 0.8 select_reduce_fusion.2
  195.0 14.7 %all_gather.12 = bf16[256,5,128]{2,0,1:T(8,128)(2,1)S(1)} all-gather(bf16[64,5,128]{2,0,1:T(8,128)(2,1)S(1)} %copy.100), channel_id=1, replica_groups=mesh['outer'=8,'inner'=4] {'inner'}, dimensions={0}, use_global_device_ids=true | all-gather | bytes 409600 | tf_op jit(solution)/shard_map/all_gather | solution.py:106
  209.7 14.1 %all_gather.13 = bf16[256,5,128]{2,0,1:T(8,128)(2,1)S(1)} all-gather(bf16[64,5,128]{2,0,1:T(8,128)(2,1)S(1)} %copy.102), channel_id=1, replica_groups=mesh['outer'=8,'inner'=4] {'inner'}, dimensions={0}, use_global_device_ids=true | all-gather | bytes 409600 | tf_op jit(solution)/shard_map/all_gather | solution.py:107
  224.3 0.9 fusion.73
  225.2 1.5 convolution_bitcast_fusion.2
  226.6 1.7 convolution_bitcast_fusion.1
  229.9 1.3 copy.122
  231.1 44.7 %all-reduce.5 = bf16[256,2,5,128]{3,1,2,0:T(2,128)(2,1)S(1)} all-reduce(f32[256,2,5,128]{3,1,2,0:T(2,128)S(1)} %copy.122), channel_id=2, replica_groups=mesh['outer'=8,'inner'=4] {'inner'}, use_global_device_ids=true, to_apply=%region_17.18.clone | all-reduce | flops 327680 | bytes 1966080
  276.9 1.5 fusion.74
  279.2 2.0 convolution_convert_fusion.2
  281.2 2.0 convolution_convert_fusion
  285.0 0.9 pad_maximum_fusion.3
  286.0 0.9 pad_maximum_fusion.1
  287.0 0.9 pad_maximum_fusion.2
  (86 shorter events, 13.6 us)
Async XLA Ops:
  0.6 4.6 %slice-start.2 = ((bf16[256,1536]{1,0:T(8,128)(2,1)}), bf16[256,384]{1,0:T(8,128)(2,1)S(1)}, s32[]{:S(2)}) async-start(bf16[256,1536]{1,0:T(8,128)(2,1)} %param.6), calls=%async_computation.2 | async-start | bytes 393216 | tf_op jit(solution)/shard_map/slice | solution.py:98
  4.0 1.4 slice-start.5
  5.2 0.9 slice-start.8
  8.5 178.6 %slice-start = ((bf16[256,1536]{1,0:T(8,128)(2,1)}), bf16[256,512]{1,0:T(8,128)(2,1)S(1)}, s32[]{:S(2)}) async-start(bf16[256,1536]{1,0:T(8,128)(2,1)} %param.5), calls=%async_computation | async-start | bytes 524288 | tf_op jit(solution)/shard_map/slice | solution.py:119
  144.1 43.9 %slice-start.3 = ((bf16[256,1536]{1,0:T(8,128)(2,1)}), bf16[256,512]{1,0:T(8,128)(2,1)S(1)}, s32[]{:S(2)}) async-start(bf16[256,1536]{1,0:T(8,128)(2,1)} %param.6), calls=%async_computation.3 | async-start | bytes 524288 | tf_op jit(solution)/shard_map/slice | solution.py:120
  187.1 1.7 slice-start.6
  188.0 1.0 slice-start.9
  190.7 1.2 slice-start.1
  191.8 1.0 slice-start.4
  192.0 1.2 slice-start.7
  192.8 1.0 slice-start.10
  194.9 29.4 %copy-start.2 = (bf16[64,5,128]{2,1,0:T(8,128)(2,1)}, bf16[64,5,128]{2,1,0:T(8,128)(2,1)S(1)}, u32[]{:S(2)}) copy-start(bf16[64,5,128]{2,1,0:T(8,128)(2,1)S(1)} %get-tuple-element.4) | copy-start | bytes 245764
  226.6 2.4 copy-start.3
  275.9 1.0 copy-start.4
  275.9 1.0 copy-start.5
  283.2 0.9 copy-start.1
  284.1 0.9 copy-start
where the time goes:
time: 288 us
  blocking collectives  250 us (87%)
  local copies, waits for them, and re-layouts  14.6 us (5%)
  matrix products  12.4 us (4%)
  other arithmetic  9.24 us (3%)
    unnamed x2, blocking collectives  87.1 us
    all_gather x1, blocking collectives, body(): lax.all_gather(wide_key, ('outer', 'inner'), axis=0, tiled=True)  70.2 us
    all_gather x1, blocking collectives, body(): lax.all_gather(wide_value, ('outer', 'inner'), axis=0, tiled=True)  63.8 us
    all_gather x1, blocking collectives, body(): lax.all_gather(mid_key, 'inner', axis=0, tiled=True)  14.7 us
    all_gather x1, blocking collectives, body(): lax.all_gather(mid_value, 'inner', axis=0, tiled=True)  14.1 us
    dot_general x6, matrix products, key_grad(): jnp.einsum('wfl,fwp->lwp', gradients_bfloat, query_row_block, preferred_e...  5.84 us

commit v1 on v0

v1 whole, which is shorter than its diff:
```python
import functools
import math

import jax
import jax.numpy as jnp
from jax import lax
from jax.experimental import pallas as pl
from jax.experimental.pallas import tpu as pltpu
from jax.sharding import PartitionSpec as P

HEAD_DIM = 128
H_NEAR = 4
H_MID = 5
H_WIDE = 3
HEADS = H_NEAR + H_MID + H_WIDE
R_MID = 4
R_WIDE = 128
NEAR_END = H_NEAR * HEAD_DIM
MID_END = NEAR_END + H_MID * HEAD_DIM
WIDE_ROWS = 8
MESH = pl.DeviceIdType.MESH
F32 = jnp.float32
BF16 = jnp.bfloat16


def dot(left, right, contract):
    return lax.dot_general(left, right, ((contract[:1], contract[1:]), ((), ())), preferred_element_type=F32)


def attention_parts(q, k, v, g, mask=None):
    scale = 1.0 / math.sqrt(HEAD_DIM)
    scores = dot(q, k, (1, 1)) * scale
    if mask is not None:
        scores = jnp.where(mask, scores, -1e30)
    exponent = jnp.exp(scores - jnp.max(scores, axis=1, keepdims=True))
    weights = exponent * (1.0 / jnp.sum(exponent, axis=1, keepdims=True))
    dots = dot(g, v, (1, 1))
    row_dots = jnp.sum(weights * dots, axis=1, keepdims=True)
    score_grads = (weights * (dots - row_dots) * scale).astype(BF16)
    return weights.astype(BF16), score_grads


def kernel(
    n_outer, n_inner, offsets, queries, key_rows, values, out_grads, grad_q, grad_k, grad_v,
    x, y, picked, arrived, result, returned, wide, wide_result,
    in_sem, out_sem, mid_send, mid_recv, back_send, back_recv,
    line_send, line_recv, plane_send, plane_recv,
):
    tokens = x.shape[1]
    rows = tokens // R_MID
    wide_tokens = tokens // R_WIDE
    slots = arrived.shape[0]
    me_o, me_i = lax.axis_index("outer"), lax.axis_index("inner")
    inputs = (queries, key_rows, values, out_grads)
    outputs = (grad_q, grad_k, grad_v)

    def inner_peer(step):
        return lax.rem(me_i + step, n_inner)

    def outer_peer(step):
        return lax.rem(me_o + step, n_outer)

    spans = (pl.ds(NEAR_END, HEADS * HEAD_DIM - NEAR_END), pl.ds(0, NEAR_END))
    loads = [
        [
            pltpu.make_async_copy(inputs[a].at[:, span], x.at[a, :, span], in_sem.at[s, a])
            for a in range(4)
        ]
        for s, span in enumerate(spans)
    ]
    for group in loads:
        for load in group:
            load.start()

    barrier = pltpu.get_barrier_semaphore()
    for step in range(1, n_inner):
        pl.semaphore_signal(barrier, inc=1, device_id=(me_o, inner_peer(step)), device_id_type=MESH)
    for step in range(1, n_outer):
        pl.semaphore_signal(barrier, inc=1, device_id=(outer_peer(step), me_i), device_id_type=MESH)

    for load in loads[0]:
        load.wait()

    position = lax.broadcasted_iota(jnp.int32, (16, tokens), 1)
    row = lax.broadcasted_iota(jnp.int32, (16, tokens), 0)
    chosen = jnp.zeros((16, tokens), jnp.bool_)
    for head in range(H_WIDE):
        for token in range(wide_tokens):
            at = token * R_WIDE + offsets[H_MID + head]
            chosen = chosen | ((row == head * wide_tokens + token) & (position == at))
    chosen = chosen.astype(F32).astype(BF16)
    head_of = lax.broadcasted_iota(jnp.int32, (WIDE_ROWS, HEAD_DIM), 0) // wide_tokens
    blocks = []
    for a in range(4):
        both = dot(chosen, x[a, :, MID_END:], (1, 0))[:WIDE_ROWS]
        block = jnp.zeros((WIDE_ROWS, HEAD_DIM), F32)
        for head in range(H_WIDE):
            part = both[:, head * HEAD_DIM:(head + 1) * HEAD_DIM]
            block = jnp.where(head_of == head, part, block)
        blocks.append(block)
    wide[me_o, me_i] = jnp.concatenate(blocks, axis=0).astype(BF16)

    pl.semaphore_wait(barrier, n_inner - 1 + n_outer - 1)

    def line_copy(step, source):
        return pltpu.make_async_remote_copy(
            src_ref=wide.at[me_o, me_i], dst_ref=wide.at[me_o, source],
            send_sem=line_send.at[step], recv_sem=line_recv.at[source],
            device_id=(me_o, inner_peer(step)), device_id_type=MESH,
        )

    for step in range(1, n_inner):
        line_copy(step, me_i).start()

    def owner(head):
        if head < n_inner:
            return jnp.int32(head)
        return lax.rem(head % n_inner + n_inner // 2 + n_inner - lax.rem(me_o, 2), n_inner)

    def mid_copy(head, slot, source, target):
        return pltpu.make_async_remote_copy(
            src_ref=picked.at[head], dst_ref=arrived.at[slot, source],
            send_sem=mid_send.at[head], recv_sem=mid_recv.at[slot, source],
            device_id=(me_o, target), device_id_type=MESH,
        )

    pick_row = lax.broadcasted_iota(jnp.int32, (rows, tokens), 0)
    pick_position = lax.broadcasted_iota(jnp.int32, (rows, tokens), 1)
    for head in range(H_MID):
        pick = (pick_position == pick_row * R_MID + offsets[head]).astype(F32).astype(BF16)
        columns = slice(NEAR_END + head * HEAD_DIM, NEAR_END + (head + 1) * HEAD_DIM)
        for a in range(4):
            picked[head, a] = dot(pick, x[a, :, columns], (1, 0)).astype(BF16)
        target = owner(head)

        @pl.when(me_i != target)
        def _():
            mid_copy(head, head // n_inner, me_i, target).start()

        @pl.when(me_i == target)
        def _():
            arrived[head // n_inner, me_i] = picked[head]

    for load in loads[1]:
        load.wait()

    def near_head(head, carry):
        columns = pl.ds(pl.multiple_of(head * HEAD_DIM, HEAD_DIM), HEAD_DIM)
        q, k, v, g = [x[a, :, columns] for a in range(4)]
        weights, score_grads = attention_parts(q, k, v, g)
        y[0, :, columns] = dot(score_grads, k, (1, 0)).astype(BF16)
        y[1, :, columns] = dot(score_grads, q, (0, 0)).astype(BF16)
        y[2, :, columns] = dot(weights, g, (0, 0)).astype(BF16)
        return carry

    lax.fori_loop(0, H_NEAR // 2, near_head, 0)

    for step in range(1, n_inner):
        line_copy(step, inner_peer(step)).wait_recv()

    def plane_copy(step, source):
        return pltpu.make_async_remote_copy(
            src_ref=wide.at[me_o], dst_ref=wide.at[source],
            send_sem=plane_send.at[step], recv_sem=plane_recv.at[source],
            device_id=(outer_peer(step), me_i), device_id_type=MESH,
        )

    for step in range(1, n_outer):
        plane_copy(step, me_o).start()

    lax.fori_loop(H_NEAR // 2, H_NEAR, near_head, 0)

    def store(group, span):
        return [
            pltpu.make_async_copy(y.at[which, :, span], outputs[which].at[:, span], out_sem.at[group, which])
            for which in range(3)
        ]

    stores = store(0, spans[1])
    for copy in stores:
        copy.start()

    for step in range(1, n_outer):
        plane_copy(step, outer_peer(step)).wait_recv()
    devices = n_outer * n_inner
    total = devices * WIDE_ROWS
    tile = min(total, 256)

    def gathered(a, start, count):
        block = wide[...].reshape(devices, 4 * WIDE_ROWS, HEAD_DIM).astype(F32)
        return block[start:start + count, a * WIDE_ROWS:(a + 1) * WIDE_ROWS].reshape(
            count * WIDE_ROWS, HEAD_DIM).astype(BF16)

    wide_k, wide_v = gathered(1, 0, devices), gathered(2, 0, devices)
    wide_result[...] = jnp.zeros_like(wide_result)
    for first in range(0, total, tile):
        q = gathered(0, first // WIDE_ROWS, tile // WIDE_ROWS)
        g = gathered(3, first // WIDE_ROWS, tile // WIDE_ROWS)
        query_head = lax.rem(lax.broadcasted_iota(jnp.int32, (tile, total), 0), WIDE_ROWS) // wide_tokens
        key_head = lax.rem(lax.broadcasted_iota(jnp.int32, (tile, total), 1), WIDE_ROWS) // wide_tokens
        weights, score_grads = attention_parts(q, wide_k, wide_v, g, query_head == key_head)
        wide_result[0, first:first + tile] = dot(score_grads, wide_k, (1, 0))
        wide_result[1] += dot(score_grads, q, (0, 0))
        wide_result[2] += dot(weights, g, (0, 0))
    mine = pl.ds(pl.multiple_of((me_o * n_inner + me_i) * WIDE_ROWS, WIDE_ROWS), WIDE_ROWS)
    place = lax.broadcasted_iota(jnp.int32, (tokens, HEAD_DIM), 0)
    for which in range(3):
        block = wide_result[which, mine, :]
        for head in range(H_WIDE):
            spread = jnp.zeros((tokens, HEAD_DIM), F32)
            for token in range(wide_tokens):
                at = head * wide_tokens + token
                spread = jnp.where(
                    place == token * R_WIDE + offsets[H_MID + head], block[at:at + 1], spread
                )
            first = MID_END + head * HEAD_DIM
            y[which, :, first:first + HEAD_DIM] = spread.astype(BF16)

    def back_copy(slot, head, source):
        return pltpu.make_async_remote_copy(
            src_ref=result.at[slot, source], dst_ref=returned.at[head],
            send_sem=back_send.at[slot, source], recv_sem=back_recv.at[head],
            device_id=(me_o, source), device_id_type=MESH,
        )

    def owned(slot):
        if slot == 0:
            return me_i
        shift = lax.rem(me_i + 2 * n_inner - n_inner // 2 + lax.rem(me_o, 2), n_inner)
        return slot * n_inner + shift

    segment = n_inner * rows
    for slot in range(slots):
        head = owned(slot)

        @pl.when(head < H_MID)
        def _():
            for step in range(1, n_inner):
                source = inner_peer(step)
                mid_copy(0, slot, source, source).wait_recv()
            q, k, v, g = [arrived[slot, :, a].reshape(segment, HEAD_DIM) for a in range(4)]
            weights, score_grads = attention_parts(q, k, v, g)
            grads = (
                dot(score_grads, k, (1, 0)), dot(score_grads, q, (0, 0)), dot(weights, g, (0, 0))
            )
            for which in range(3):
                result[slot, :, which] = grads[which].astype(BF16).reshape(n_inner, rows, HEAD_DIM)
            for step in range(1, n_inner):
                back_copy(slot, head, inner_peer(step)).start()
            returned[head] = result[slot, me_i]

    spread_row = lax.broadcasted_iota(jnp.int32, (tokens, rows), 1)
    spread_position = lax.broadcasted_iota(jnp.int32, (tokens, rows), 0)
    for head in range(H_MID):
        target = owner(head)

        @pl.when(me_i != target)
        def _():
            back_copy(0, head, target).wait_recv()

        place = (spread_position == spread_row * R_MID + offsets[head]).astype(F32).astype(BF16)
        columns = slice(NEAR_END + head * HEAD_DIM, NEAR_END + (head + 1) * HEAD_DIM)
        for which in range(3):
            y[which, :, columns] = dot(place, returned[head, which], (1, 0)).astype(BF16)

    last = store(1, spans[0])
    for copy in last:
        copy.start()

    for step in range(1, n_inner):
        line_copy(step, me_i).wait_send()
    for step in range(1, n_outer):
        plane_copy(step, me_o).wait_send()
    for head in range(H_MID):
        target = owner(head)

        @pl.when(me_i != target)
        def _():
            mid_copy(head, 0, me_i, target).wait_send()

    for slot in range(slots):
        head = owned(slot)

        @pl.when(head < H_MID)
        def _():
            for step in range(1, n_inner):
                back_copy(slot, head, inner_peer(step)).wait_send()

    for copy in stores + last:
        copy.wait()


def body(n_outer, n_inner, queries, key_rows, values, out_grads, offsets):
    tokens, columns = queries.shape
    rows = tokens // R_MID
    slots = -(-H_MID // n_inner)
    anywhere = pl.BlockSpec(memory_space=pl.ANY)
    dma = pltpu.SemaphoreType.DMA
    return tuple(pl.pallas_call(
        functools.partial(kernel, n_outer, n_inner),
        out_shape=[jax.ShapeDtypeStruct((tokens, columns), BF16)] * 3,
        in_specs=[pl.BlockSpec(memory_space=pltpu.SMEM)] + [anywhere] * 4,
        out_specs=[anywhere] * 3,
        scratch_shapes=[
            pltpu.VMEM((4, tokens, columns), BF16),
            pltpu.VMEM((3, tokens, columns), BF16),
            pltpu.VMEM((H_MID, 4, rows, HEAD_DIM), BF16),
            pltpu.VMEM((slots, n_inner, 4, rows, HEAD_DIM), BF16),
            pltpu.VMEM((slots, n_inner, 3, rows, HEAD_DIM), BF16),
            pltpu.VMEM((H_MID, 3, rows, HEAD_DIM), BF16),
            pltpu.VMEM((n_outer, n_inner, 4 * WIDE_ROWS, HEAD_DIM), BF16),
            pltpu.VMEM((3, n_outer * n_inner * WIDE_ROWS, HEAD_DIM), F32),
            dma((2, 4)),
            dma((2, 3)),
            dma((H_MID,)),
            dma((slots, n_inner)),
            dma((slots, n_inner)),
            dma((H_MID,)),
            dma((n_inner,)),
            dma((n_inner,)),
            dma((n_outer,)),
            dma((n_outer,)),
        ],
        compiler_params=pltpu.CompilerParams(
            collective_id=0, has_side_effects=True, vmem_limit_bytes=48 * 1024 * 1024
        ),
    )(offsets, queries, key_rows, values, out_grads))


def solution(mesh):
    split = P(("outer", "inner"), None)
    return jax.shard_map(
        functools.partial(body, mesh.shape["outer"], mesh.shape["inner"]),
        mesh=mesh,
        in_specs=(split, split, split, split, P()),
        out_specs=(split,) * 3,
        check_vma=False,
    )
```

time: 288 us -> 32.5 us (0.11)
  blocking collectives: 250 us -> 0 us
  Pallas kernels: 0 us -> 23.7 us
  matrix products: 12.4 us -> 0 us
  other arithmetic: 9.24 us -> 0 us
  local copies, waits for them, and re-layouts: 14.6 us -> 7.82 us
    all_gather x4 -> x0, blocking collectives: 163 us -> none  [the longest x1 70.2 us: body(): lax.all_gather(wide_key, ('outer', 'inner'), axis=0, tiled=True)]
    unnamed x2 -> x0, blocking collectives: 87.1 us -> none
    pallas_call x0 -> x1, Pallas kernels: none -> 23.7 us  [body(): pl.pallas_call(functools.partial(kernel, n_outer, n_inner), out_shape=[ja...]
    dot_general x13 -> x0, matrix products: 10.6 us -> none  [the longest x6 5.84 us: key_grad(): jnp.einsum('wfl,fwp->lwp', gradients_bfloat, query_row_block, preferred_e...]
    slice x29 -> x0, local copies, waits for them, and re-layouts: 3.72 us -> none  [the longest x2 1.13 us: body(): wide_query = select_rows(queries[:, mid_end:], wide_offsets, R_WIDE)]
    unnamed x23 -> x13, local copies, waits for them, and re-layouts: 4.77 us -> 7.82 us
where the time goes in v1:
time: 32.5 us; the launch traced here: 32.2 us
  Pallas kernels  23.7 us (73%)
  local copies, waits for them, and re-layouts  7.82 us (24%)
  between operations  0.65 us (2%)
    pallas_call x1, Pallas kernels, body(): pl.pallas_call(functools.partial(kernel, n_outer, n_inner), out_shape=[ja...  23.7 us
    unnamed x13, local copies, waits for them, and re-layouts  7.82 us

profile of v1, /device:TPU:0, one launch (start us, length us, event | category | flops | bytes accessed | tf_op | source)
XLA Modules:
  0.0 32.2 jit_solution(3256278187346915585)
XLA Ops:
  0.6 0.0 copy-start
  0.6 1.1 %copy-done = bf16[256,1536]{1,0:T(8,128)(2,1)S(1)} copy-done((bf16[256,1536]{1,0:T(8,128)(2,1)S(1)}, bf16[256,1536]{1,0:T(8,128)(2,1)}, u32[]{:S(2)}) %copy-start) | copy-done | bytes 786456
  1.8 0.0 copy-start.1
  1.8 1.1 %copy-done.1 = bf16[256,1536]{1,0:T(8,128)(2,1)S(1)} copy-done((bf16[256,1536]{1,0:T(8,128)(2,1)S(1)}, bf16[256,1536]{1,0:T(8,128)(2,1)}, u32[]{:S(2)}) %copy-start.1) | copy-done | bytes 786456
  2.9 0.0 copy-start.2
  2.9 1.1 %copy-done.2 = bf16[256,1536]{1,0:T(8,128)(2,1)S(1)} copy-done((bf16[256,1536]{1,0:T(8,128)(2,1)S(1)}, bf16[256,1536]{1,0:T(8,128)(2,1)}, u32[]{:S(2)}) %copy-start.2) | copy-done | bytes 786456
  4.0 0.0 copy-start.3
  4.0 1.1 %copy-done.3 = bf16[256,1536]{1,0:T(8,128)(2,1)S(1)} copy-done((bf16[256,1536]{1,0:T(8,128)(2,1)S(1)}, bf16[256,1536]{1,0:T(8,128)(2,1)}, u32[]{:S(2)}) %copy-start.3) | copy-done | bytes 786456
  5.2 0.0 copy-start.4
  5.2 0.7 %copy-done.4 = s32[8]{0:T(128)S(1)} copy-done((s32[8]{0:T(128)S(1)}, s32[8]{0:T(128)}, u32[]{:S(2)}) %copy-start.4) | copy-done | bytes 56
  5.8 23.7 %shard_map.76 = (bf16[256,1536]{1,0:T(8,128)(2,1)S(1)}, bf16[256,1536]{1,0:T(8,128)(2,1)S(1)}, bf16[256,1536]{1,0:T(8,128)(2,1)S(1)}) custom-call(s32[8]{0:T(128)S(1)} %copy-done.4, bf16[256,1536]{1,0:T(8,128)(2,1)S(1)} %copy-done, bf16[256,1536]{1,0:T(8,128)(2,1)S(1)} %copy-done.1, bf16[256,1536]{1,0:T(8,128)(2,1)S(1)} %copy-done.2, ...), custom_call_target="tpu_custom_call" | custom-call | tf_op jit(solution)/shard_map/pallas_call | solution.py:299
  29.5 0.9 %copy.11 = bf16[256,1536]{1,0:T(8,128)(2,1)} copy(bf16[256,1536]{1,0:T(8,128)(2,1)S(1)} %get-tuple-element.6) | data formatting | bytes 1572864
  30.4 0.9 %copy.12 = bf16[256,1536]{1,0:T(8,128)(2,1)} copy(bf16[256,1536]{1,0:T(8,128)(2,1)S(1)} %get-tuple-element.7) | data formatting | bytes 1572864
  31.3 0.9 %copy.13 = bf16[256,1536]{1,0:T(8,128)(2,1)} copy(bf16[256,1536]{1,0:T(8,128)(2,1)S(1)} %get-tuple-element.8) | data formatting | bytes 1572864
Async XLA Ops:
  0.6 1.1 %copy-start = (bf16[256,1536]{1,0:T(8,128)(2,1)S(1)}, bf16[256,1536]{1,0:T(8,128)(2,1)}, u32[]{:S(2)}) copy-start(bf16[256,1536]{1,0:T(8,128)(2,1)} %queries.1) | copy-start | bytes 2359300
  1.8 1.1 %copy-start.1 = (bf16[256,1536]{1,0:T(8,128)(2,1)S(1)}, bf16[256,1536]{1,0:T(8,128)(2,1)}, u32[]{:S(2)}) copy-start(bf16[256,1536]{1,0:T(8,128)(2,1)} %key_rows.1) | copy-start | bytes 2359300
  2.9 1.1 %copy-start.2 = (bf16[256,1536]{1,0:T(8,128)(2,1)S(1)}, bf16[256,1536]{1,0:T(8,128)(2,1)}, u32[]{:S(2)}) copy-start(bf16[256,1536]{1,0:T(8,128)(2,1)} %values.1) | copy-start | bytes 2359300
  4.0 1.1 %copy-start.3 = (bf16[256,1536]{1,0:T(8,128)(2,1)S(1)}, bf16[256,1536]{1,0:T(8,128)(2,1)}, u32[]{:S(2)}) copy-start(bf16[256,1536]{1,0:T(8,128)(2,1)} %out_grads.1) | copy-start | bytes 2359300
  5.2 0.7 %copy-start.4 = (s32[8]{0:T(128)S(1)}, s32[8]{0:T(128)}, u32[]{:S(2)}) copy-start(s32[8]{0:T(128)} %offsets.1) | copy-start | bytes 100

commit v2 on v1

--- a/solution.py
+++ b/solution.py
@@ -41,9 +41,9 @@
 
 
 def kernel(
-    n_outer, n_inner, offsets, queries, key_rows, values, out_grads, grad_q, grad_k, grad_v,
-    x, y, picked, arrived, result, returned, wide, wide_result,
-    in_sem, out_sem, mid_send, mid_recv, back_send, back_recv,
+    n_outer, n_inner, offsets_in, queries, key_rows, values, out_grads, grad_q, grad_k, grad_v,
+    offsets, x, y, picked, arrived, result, returned, wide, wide_result,
+    offsets_sem, in_sem, out_sem, mid_send, mid_recv, back_send, back_recv,
     line_send, line_recv, plane_send, plane_recv,
 ):
     tokens = x.shape[1]
@@ -60,17 +60,28 @@
     def outer_peer(step):
         return lax.rem(me_o + step, n_outer)
 
-    spans = (pl.ds(NEAR_END, HEADS * HEAD_DIM - NEAR_END), pl.ds(0, NEAR_END))
-    loads = [
-        [
-            pltpu.make_async_copy(inputs[a].at[:, span], x.at[a, :, span], in_sem.at[s, a])
+    first_head = jnp.where(me_i < n_inner // 2, n_inner // 2, n_inner)
+
+    def head_at(step):
+        return lax.rem(first_head + step, H_MID)
+
+    def head_columns(head):
+        return pl.ds(pl.multiple_of(NEAR_END + head * HEAD_DIM, HEAD_DIM), HEAD_DIM)
+
+    def load(group, span):
+        return [
+            pltpu.make_async_copy(inputs[a].at[:, span], x.at[a, :, span], in_sem.at[group, a])
             for a in range(4)
         ]
-        for s, span in enumerate(spans)
-    ]
+
+    near_span, wide_span = pl.ds(0, NEAR_END), pl.ds(MID_END, H_WIDE * HEAD_DIM)
+    offsets_load = pltpu.make_async_copy(offsets_in, offsets, offsets_sem)
+    offsets_load.start()
+    loads = [load(step, head_columns(head_at(step))) for step in range(H_MID)]
+    loads += [load(H_MID, wide_span), load(H_MID + 1, near_span)]
     for group in loads:
-        for load in group:
-            load.start()
+        for copy in group:
+            copy.start()
 
     barrier = pltpu.get_barrier_semaphore()
     for step in range(1, n_inner):
@@ -78,9 +89,49 @@
     for step in range(1, n_outer):
         pl.semaphore_signal(barrier, inc=1, device_id=(outer_peer(step), me_i), device_id_type=MESH)
 
-    for load in loads[0]:
-        load.wait()
-
+    def owner(head):
+        turned = head + n_inner // 2 + n_inner - lax.rem(me_o, 2)
+        return jnp.where(head < n_inner, head, lax.rem(turned, n_inner))
+
+    def mid_copy(head, slot, source, target):
+        return pltpu.make_async_remote_copy(
+            src_ref=picked.at[head], dst_ref=arrived.at[slot, source],
+            send_sem=mid_send.at[head], recv_sem=mid_recv.at[slot, source],
+            device_id=(me_o, target), device_id_type=MESH,
+        )
+
+    pick_row = lax.broadcasted_iota(jnp.int32, (rows, tokens), 0)
+    pick_position = lax.broadcasted_iota(jnp.int32, (rows, tokens), 1)
+
+    def pick_head(step):
+        for copy in loads[step]:
+            copy.wait()
+        head = head_at(step)
+        pick = (pick_position == pick_row * R_MID + offsets[head]).astype(F32).astype(BF16)
+        for a in range(4):
+            picked[head, a] = dot(pick, x[a, :, head_columns(head)], (1, 0)).astype(BF16)
+
+    def send_head(step):
+        head = head_at(step)
+        target, slot = owner(head), head // n_inner
+
+        @pl.when(me_i != target)
+        def _():
+            mid_copy(head, slot, me_i, target).start()
+
+        @pl.when(me_i == target)
+        def _():
+            arrived[slot, me_i] = picked[head]
+
+    offsets_load.wait()
+    pick_head(0)
+    pl.semaphore_wait(barrier, n_inner - 1 + n_outer - 1)
+    send_head(0)
+    pick_head(1)
+    send_head(1)
+
+    for copy in loads[H_MID]:
+        copy.wait()
     position = lax.broadcasted_iota(jnp.int32, (16, tokens), 1)
     row = lax.broadcasted_iota(jnp.int32, (16, tokens), 0)
     chosen = jnp.zeros((16, tokens), jnp.bool_)
@@ -100,8 +151,6 @@
         blocks.append(block)
     wide[me_o, me_i] = jnp.concatenate(blocks, axis=0).astype(BF16)
 
-    pl.semaphore_wait(barrier, n_inner - 1 + n_outer - 1)
-
     def line_copy(step, source):
         return pltpu.make_async_remote_copy(
             src_ref=wide.at[me_o, me_i], dst_ref=wide.at[me_o, source],
@@ -112,48 +161,23 @@
     for step in range(1, n_inner):
         line_copy(step, me_i).start()
 
-    def owner(head):
-        if head < n_inner:
-            return jnp.int32(head)
-        return lax.rem(head % n_inner + n_inner // 2 + n_inner - lax.rem(me_o, 2), n_inner)
-
-    def mid_copy(head, slot, source, target):
-        return pltpu.make_async_remote_copy(
-            src_ref=picked.at[head], dst_ref=arrived.at[slot, source],
-            send_sem=mid_send.at[head], recv_sem=mid_recv.at[slot, source],
-            device_id=(me_o, target), device_id_type=MESH,
-        )
-
-    pick_row = lax.broadcasted_iota(jnp.int32, (rows, tokens), 0)
-    pick_position = lax.broadcasted_iota(jnp.int32, (rows, tokens), 1)
-    for head in range(H_MID):
-        pick = (pick_position == pick_row * R_MID + offsets[head]).astype(F32).astype(BF16)
-        columns = slice(NEAR_END + head * HEAD_DIM, NEAR_END + (head + 1) * HEAD_DIM)
-        for a in range(4):
-            picked[head, a] = dot(pick, x[a, :, columns], (1, 0)).astype(BF16)
-        target = owner(head)
-
-        @pl.when(me_i != target)
-        def _():
-            mid_copy(head, head // n_inner, me_i, target).start()
-
-        @pl.when(me_i == target)
-        def _():
-            arrived[head // n_inner, me_i] = picked[head]
-
-    for load in loads[1]:
-        load.wait()
-
-    def near_head(head, carry):
-        columns = pl.ds(pl.multiple_of(head * HEAD_DIM, HEAD_DIM), HEAD_DIM)
+    for step in range(2, H_MID):
+        pick_head(step)
+        send_head(step)
+
+    for copy in loads[H_MID + 1]:
+        copy.wait()
+
+    def near_head(head):
+        columns = slice(head * HEAD_DIM, (head + 1) * HEAD_DIM)
         q, k, v, g = [x[a, :, columns] for a in range(4)]
         weights, score_grads = attention_parts(q, k, v, g)
         y[0, :, columns] = dot(score_grads, k, (1, 0)).astype(BF16)
         y[1, :, columns] = dot(score_grads, q, (0, 0)).astype(BF16)
         y[2, :, columns] = dot(weights, g, (0, 0)).astype(BF16)
-        return carry
-
-    lax.fori_loop(0, H_NEAR // 2, near_head, 0)
+
+    for head in range(H_NEAR // 2):
+        near_head(head)
 
     for step in range(1, n_inner):
         line_copy(step, inner_peer(step)).wait_recv()
@@ -168,7 +192,41 @@
     for step in range(1, n_outer):
         plane_copy(step, me_o).start()
 
-    lax.fori_loop(H_NEAR // 2, H_NEAR, near_head, 0)
+    def back_copy(slot, head, source):
+        return pltpu.make_async_remote_copy(
+            src_ref=result.at[slot, source], dst_ref=returned.at[head],
+            send_sem=back_send.at[slot, source], recv_sem=back_recv.at[head],
+            device_id=(me_o, source), device_id_type=MESH,
+        )
+
+    def owned(slot):
+        if slot == 0:
+            return me_i
+        shift = lax.rem(me_i + 2 * n_inner - n_inner // 2 + lax.rem(me_o, 2), n_inner)
+        return slot * n_inner + shift
+
+    segment = n_inner * rows
+    for slot in range(slots):
+        head = owned(slot)
+
+        @pl.when(head < H_MID)
+        def _():
+            for step in range(1, n_inner):
+                source = inner_peer(step)
+                mid_copy(0, slot, source, source).wait_recv()
+            q, k, v, g = [arrived[slot, :, a].reshape(segment, HEAD_DIM) for a in range(4)]
+            weights, score_grads = attention_parts(q, k, v, g)
+            grads = (
+                dot(score_grads, k, (1, 0)), dot(score_grads, q, (0, 0)), dot(weights, g, (0, 0))
+            )
+            for which in range(3):
+                result[slot, :, which] = grads[which].astype(BF16).reshape(n_inner, rows, HEAD_DIM)
+            for step in range(1, n_inner):
+                back_copy(slot, head, inner_peer(step)).start()
+            returned[head] = result[slot, me_i]
+
+    for head in range(H_NEAR // 2, H_NEAR):
+        near_head(head)
 
     def store(group, span):
         return [
@@ -176,7 +234,7 @@
             for which in range(3)
         ]
 
-    stores = store(0, spans[1])
+    stores = store(H_MID, near_span)
     for copy in stores:
         copy.start()
 
@@ -216,38 +274,9 @@
             first = MID_END + head * HEAD_DIM
             y[which, :, first:first + HEAD_DIM] = spread.astype(BF16)
 
-    def back_copy(slot, head, source):
-        return pltpu.make_async_remote_copy(
-            src_ref=result.at[slot, source], dst_ref=returned.at[head],
-            send_sem=back_send.at[slot, source], recv_sem=back_recv.at[head],
-            device_id=(me_o, source), device_id_type=MESH,
-        )
-
-    def owned(slot):
-        if slot == 0:
-            return me_i
-        shift = lax.rem(me_i + 2 * n_inner - n_inner // 2 + lax.rem(me_o, 2), n_inner)
-        return slot * n_inner + shift
-
-    segment = n_inner * rows
-    for slot in range(slots):
-        head = owned(slot)
-
-        @pl.when(head < H_MID)
-        def _():
-            for step in range(1, n_inner):
-                source = inner_peer(step)
-                mid_copy(0, slot, source, source).wait_recv()
-            q, k, v, g = [arrived[slot, :, a].reshape(segment, HEAD_DIM) for a in range(4)]
-            weights, score_grads = attention_parts(q, k, v, g)
-            grads = (
-                dot(score_grads, k, (1, 0)), dot(score_grads, q, (0, 0)), dot(weights, g, (0, 0))
-            )
-            for which in range(3):
-                result[slot, :, which] = grads[which].astype(BF16).reshape(n_inner, rows, HEAD_DIM)
-            for step in range(1, n_inner):
-                back_copy(slot, head, inner_peer(step)).start()
-            returned[head] = result[slot, me_i]
+    stores += store(H_MID + 1, wide_span)
+    for copy in stores[-3:]:
+        copy.start()
 
     spread_row = lax.broadcasted_iota(jnp.int32, (tokens, rows), 1)
     spread_position = lax.broadcasted_iota(jnp.int32, (tokens, rows), 0)
@@ -259,13 +288,12 @@
             back_copy(0, head, target).wait_recv()
 
         place = (spread_position == spread_row * R_MID + offsets[head]).astype(F32).astype(BF16)
-        columns = slice(NEAR_END + head * HEAD_DIM, NEAR_END + (head + 1) * HEAD_DIM)
+        columns = pl.ds(NEAR_END + head * HEAD_DIM, HEAD_DIM)
         for which in range(3):
             y[which, :, columns] = dot(place, returned[head, which], (1, 0)).astype(BF16)
-
-    last = store(1, spans[0])
-    for copy in last:
-        copy.start()
+        stores += store(head, columns)
+        for copy in stores[-3:]:
+            copy.start()
 
     for step in range(1, n_inner):
         line_copy(step, me_i).wait_send()
@@ -286,8 +314,35 @@
             for step in range(1, n_inner):
                 back_copy(slot, head, inner_peer(step)).wait_send()
 
-    for copy in stores + last:
+    for copy in stores:
         copy.wait()
+
+
+def write_out(grads):
+    pieces = 4
+
+    def copies(*refs):
+        sems = refs[6]
+        step = refs[0].shape[0] // pieces
+        started = []
+        for which in range(3):
+            for piece in range(pieces):
+                part = pl.ds(piece * step, step)
+                copy = pltpu.make_async_copy(
+                    refs[which].at[part], refs[3 + which].at[part], sems.at[which, piece]
+                )
+                copy.start()
+                started.append(copy)
+        for copy in started:
+            copy.wait()
+
+    return tuple(pl.pallas_call(
+        copies,
+        out_shape=[jax.ShapeDtypeStruct(grad.shape, grad.dtype) for grad in grads],
+        in_specs=[pl.BlockSpec(memory_space=pl.ANY)] * 3,
+        out_specs=[pl.BlockSpec(memory_space=pltpu.HBM)] * 3,
+        scratch_shapes=[pltpu.SemaphoreType.DMA((3, pieces))],
+    )(*grads))
 
 
 def body(n_outer, n_inner, queries, key_rows, values, out_grads, offsets):
@@ -296,12 +351,13 @@
     slots = -(-H_MID // n_inner)
     anywhere = pl.BlockSpec(memory_space=pl.ANY)
     dma = pltpu.SemaphoreType.DMA
-    return tuple(pl.pallas_call(
+    grads = pl.pallas_call(
         functools.partial(kernel, n_outer, n_inner),
         out_shape=[jax.ShapeDtypeStruct((tokens, columns), BF16)] * 3,
-        in_specs=[pl.BlockSpec(memory_space=pltpu.SMEM)] + [anywhere] * 4,
+        in_specs=[pl.BlockSpec(memory_space=pltpu.HBM)] * 5,
         out_specs=[anywhere] * 3,
         scratch_shapes=[
+            pltpu.SMEM(offsets.shape, jnp.int32),
             pltpu.VMEM((4, tokens, columns), BF16),
             pltpu.VMEM((3, tokens, columns), BF16),
             pltpu.VMEM((H_MID, 4, rows, HEAD_DIM), BF16),
@@ -310,8 +366,9 @@
             pltpu.VMEM((H_MID, 3, rows, HEAD_DIM), BF16),
             pltpu.VMEM((n_outer, n_inner, 4 * WIDE_ROWS, HEAD_DIM), BF16),
             pltpu.VMEM((3, n_outer * n_inner * WIDE_ROWS, HEAD_DIM), F32),
-            dma((2, 4)),
-            dma((2, 3)),
+            dma,
+            dma((H_MID + 2, 4)),
+            dma((H_MID + 2, 3)),
             dma((H_MID,)),
             dma((slots, n_inner)),
             dma((slots, n_inner)),
@@ -324,7 +381,8 @@
         compiler_params=pltpu.CompilerParams(
             collective_id=0, has_side_effects=True, vmem_limit_bytes=48 * 1024 * 1024
         ),
-    )(offsets, queries, key_rows, values, out_grads))
+    )(*[pltpu.with_memory_space_constraint(a, pltpu.HBM) for a in (offsets, queries, key_rows, values, out_grads)])
+    return write_out(grads)
 
 
 def solution(mesh):

time: 32.5 us -> 98.6 us (3.03)
  Pallas kernels: 23.7 us -> 95.2 us
  local copies, waits for them, and re-layouts: 7.82 us -> 2.67 us
    pallas_call x0 -> x1, Pallas kernels: none -> 72.7 us  [write_out(): pl.pallas_call(copies, out_shape=[jax.ShapeDtypeStruct(grad.shape, grad.d...]
    unnamed x13 -> x6, local copies, waits for them, and re-layouts: 7.82 us -> 2.67 us
    pallas_call x1, Pallas kernels: 23.7 us -> 22.5 us  [body(): pl.pallas_call(functools.partial(kernel, n_outer, n_inner), out_shape=[ja...]
where the time goes in v2:
time: 98.6 us; the launch traced here: 98.5 us
  Pallas kernels  95.2 us (97%)
  local copies, waits for them, and re-layouts  2.67 us (3%)
    pallas_call x1, Pallas kernels, write_out(): pl.pallas_call(copies, out_shape=[jax.ShapeDtypeStruct(grad.shape, grad.d...  72.7 us
    pallas_call x1, Pallas kernels, body(): pl.pallas_call(functools.partial(kernel, n_outer, n_inner), out_shape=[ja...  22.5 us
    unnamed x6, local copies, waits for them, and re-layouts  2.67 us

profile of v2, /device:TPU:0, one launch (start us, length us, event | category | flops | bytes accessed | tf_op | source)
XLA Modules:
  0.0 98.5 jit_solution(13367343060147687953)
XLA Ops:
  0.6 22.5 %shard_map.76 = (bf16[256,1536]{1,0:T(8,128)(2,1)S(1)}, bf16[256,1536]{1,0:T(8,128)(2,1)S(1)}, bf16[256,1536]{1,0:T(8,128)(2,1)S(1)}) custom-call(s32[8]{0:T(128)} %offsets_in.1, bf16[256,1536]{1,0:T(8,128)(2,1)} %queries.1, bf16[256,1536]{1,0:T(8,128)(2,1)} %key_rows.1, bf16[256,1536]{1,0:T(8,128)(2,1)} %values.1, bf16[256,1536]{1,0:T(8,128)(2,1)} %out_grads.1), custom_call_target="tpu_custom_call" | custom-call | tf_op jit(solution)/shard_map/pallas_call | solution.py:354
  23.1 0.0 copy-start
  23.1 0.9 copy-done
  24.0 0.0 copy-start.1
  24.0 0.9 copy-done.1
  24.9 0.0 copy-start.2
  24.9 0.9 copy-done.2
  25.8 72.7 %shard_map.77 = (bf16[256,1536]{1,0:T(8,128)(2,1)}, bf16[256,1536]{1,0:T(8,128)(2,1)}, bf16[256,1536]{1,0:T(8,128)(2,1)}) custom-call(bf16[256,1536]{1,0:T(8,128)(2,1)} %copy-done, bf16[256,1536]{1,0:T(8,128)(2,1)} %copy-done.1, bf16[256,1536]{1,0:T(8,128)(2,1)} %copy-done.2), custom_call_target="tpu_custom_call" | custom-call | tf_op jit(solution)/shard_map/pallas_call | solution.py:339
Async XLA Ops:
  23.1 0.9 copy-start
  24.0 0.9 copy-start.1
  24.9 0.9 copy-start.2

commit v3 on v2

--- a/solution.py
+++ b/solution.py
@@ -42,8 +42,8 @@
 
 def kernel(
     n_outer, n_inner, offsets_in, queries, key_rows, values, out_grads, grad_q, grad_k, grad_v,
-    offsets, x, y, picked, arrived, result, returned, wide, wide_result,
-    offsets_sem, in_sem, out_sem, mid_send, mid_recv, back_send, back_recv,
+    offsets, x, picked, arrived, result, returned, wide, wide_result,
+    offsets_sem, in_sem, mid_send, mid_recv, back_send, back_recv,
     line_send, line_recv, plane_send, plane_recv,
 ):
     tokens = x.shape[1]
@@ -60,10 +60,18 @@
     def outer_peer(step):
         return lax.rem(me_o + step, n_outer)
 
-    first_head = jnp.where(me_i < n_inner // 2, n_inner // 2, n_inner)
+    barrier = pltpu.get_barrier_semaphore()
+    for step in range(1, n_inner):
+        pl.semaphore_signal(barrier, inc=1, device_id=(me_o, inner_peer(step)), device_id_type=MESH)
+    for step in range(1, n_outer):
+        pl.semaphore_signal(barrier, inc=1, device_id=(outer_peer(step), me_i), device_id_type=MESH)
+
+    first_head = jnp.where(me_i < n_inner // 2, (H_MID - 1) // 2, 0)
 
     def head_at(step):
-        return lax.rem(first_head + step, H_MID)
+        if step == 0:
+            return jnp.int32(H_MID - 1)
+        return lax.rem(first_head + step - 1, H_MID - 1)
 
     def head_columns(head):
         return pl.ds(pl.multiple_of(NEAR_END + head * HEAD_DIM, HEAD_DIM), HEAD_DIM)
@@ -79,15 +87,9 @@
     offsets_load.start()
     loads = [load(step, head_columns(head_at(step))) for step in range(H_MID)]
     loads += [load(H_MID, wide_span), load(H_MID + 1, near_span)]
-    for group in loads:
-        for copy in group:
+    for group in (0, 1, H_MID, *range(2, H_MID), H_MID + 1):
+        for copy in loads[group]:
             copy.start()
-
-    barrier = pltpu.get_barrier_semaphore()
-    for step in range(1, n_inner):
-        pl.semaphore_signal(barrier, inc=1, device_id=(me_o, inner_peer(step)), device_id_type=MESH)
-    for step in range(1, n_outer):
-        pl.semaphore_signal(barrier, inc=1, device_id=(outer_peer(step), me_i), device_id_type=MESH)
 
     def owner(head):
         turned = head + n_inner // 2 + n_inner - lax.rem(me_o, 2)
@@ -172,9 +174,9 @@
         columns = slice(head * HEAD_DIM, (head + 1) * HEAD_DIM)
         q, k, v, g = [x[a, :, columns] for a in range(4)]
         weights, score_grads = attention_parts(q, k, v, g)
-        y[0, :, columns] = dot(score_grads, k, (1, 0)).astype(BF16)
-        y[1, :, columns] = dot(score_grads, q, (0, 0)).astype(BF16)
-        y[2, :, columns] = dot(weights, g, (0, 0)).astype(BF16)
+        outputs[0][:, columns] = dot(score_grads, k, (1, 0)).astype(BF16)
+        outputs[1][:, columns] = dot(score_grads, q, (0, 0)).astype(BF16)
+        outputs[2][:, columns] = dot(weights, g, (0, 0)).astype(BF16)
 
     for head in range(H_NEAR // 2):
         near_head(head)
@@ -192,10 +194,10 @@
     for step in range(1, n_outer):
         plane_copy(step, me_o).start()
 
-    def back_copy(slot, head, source):
+    def back_copy(slot, head, source, which):
         return pltpu.make_async_remote_copy(
-            src_ref=result.at[slot, source], dst_ref=returned.at[head],
-            send_sem=back_send.at[slot, source], recv_sem=back_recv.at[head],
+            src_ref=result.at[slot, source, which], dst_ref=returned.at[head, which],
+            send_sem=back_send.at[slot, source, which], recv_sem=back_recv.at[head, which],
             device_id=(me_o, source), device_id_type=MESH,
         )
 
@@ -206,7 +208,7 @@
         return slot * n_inner + shift
 
     segment = n_inner * rows
-    for slot in range(slots):
+    for slot in reversed(range(slots)):
         head = owned(slot)
 
         @pl.when(head < H_MID)
@@ -216,27 +218,17 @@
                 mid_copy(0, slot, source, source).wait_recv()
             q, k, v, g = [arrived[slot, :, a].reshape(segment, HEAD_DIM) for a in range(4)]
             weights, score_grads = attention_parts(q, k, v, g)
-            grads = (
-                dot(score_grads, k, (1, 0)), dot(score_grads, q, (0, 0)), dot(weights, g, (0, 0))
-            )
-            for which in range(3):
-                result[slot, :, which] = grads[which].astype(BF16).reshape(n_inner, rows, HEAD_DIM)
-            for step in range(1, n_inner):
-                back_copy(slot, head, inner_peer(step)).start()
-            returned[head] = result[slot, me_i]
+            for which, left, right, contract in (
+                (2, weights, g, (0, 0)), (0, score_grads, k, (1, 0)), (1, score_grads, q, (0, 0))
+            ):
+                grads = dot(left, right, contract).astype(BF16)
+                result[slot, :, which] = grads.reshape(n_inner, rows, HEAD_DIM)
+                for step in range(1, n_inner):
+                    back_copy(slot, head, inner_peer(step), which).start()
+                returned[head, which] = result[slot, me_i, which]
 
     for head in range(H_NEAR // 2, H_NEAR):
         near_head(head)
-
-    def store(group, span):
-        return [
-            pltpu.make_async_copy(y.at[which, :, span], outputs[which].at[:, span], out_sem.at[group, which])
-            for which in range(3)
-        ]
-
-    stores = store(H_MID, near_span)
-    for copy in stores:
-        copy.start()
 
     for step in range(1, n_outer):
         plane_copy(step, outer_peer(step)).wait_recv()
@@ -272,28 +264,21 @@
                     place == token * R_WIDE + offsets[H_MID + head], block[at:at + 1], spread
                 )
             first = MID_END + head * HEAD_DIM
-            y[which, :, first:first + HEAD_DIM] = spread.astype(BF16)
-
-    stores += store(H_MID + 1, wide_span)
-    for copy in stores[-3:]:
-        copy.start()
+            outputs[which][:, first:first + HEAD_DIM] = spread.astype(BF16)
 
     spread_row = lax.broadcasted_iota(jnp.int32, (tokens, rows), 1)
     spread_position = lax.broadcasted_iota(jnp.int32, (tokens, rows), 0)
     for head in range(H_MID):
         target = owner(head)
-
-        @pl.when(me_i != target)
-        def _():
-            back_copy(0, head, target).wait_recv()
-
         place = (spread_position == spread_row * R_MID + offsets[head]).astype(F32).astype(BF16)
-        columns = pl.ds(NEAR_END + head * HEAD_DIM, HEAD_DIM)
-        for which in range(3):
-            y[which, :, columns] = dot(place, returned[head, which], (1, 0)).astype(BF16)
-        stores += store(head, columns)
-        for copy in stores[-3:]:
-            copy.start()
+        columns = slice(NEAR_END + head * HEAD_DIM, NEAR_END + (head + 1) * HEAD_DIM)
+        for which in (2, 0, 1):
+
+            @pl.when(me_i != target)
+            def _():
+                back_copy(0, head, target, which).wait_recv()
+
+            outputs[which][:, columns] = dot(place, returned[head, which], (1, 0)).astype(BF16)
 
     for step in range(1, n_inner):
         line_copy(step, me_i).wait_send()
@@ -312,10 +297,8 @@
         @pl.when(head < H_MID)
         def _():
             for step in range(1, n_inner):
-                back_copy(slot, head, inner_peer(step)).wait_send()
-
-    for copy in stores:
-        copy.wait()
+                for which in range(3):
+                    back_copy(slot, head, inner_peer(step), which).wait_send()
 
 
 def write_out(grads):
@@ -339,27 +322,26 @@
     return tuple(pl.pallas_call(
         copies,
         out_shape=[jax.ShapeDtypeStruct(grad.shape, grad.dtype) for grad in grads],
-        in_specs=[pl.BlockSpec(memory_space=pl.ANY)] * 3,
+        in_specs=[pl.BlockSpec(memory_space=pltpu.VMEM)] * 3,
         out_specs=[pl.BlockSpec(memory_space=pltpu.HBM)] * 3,
         scratch_shapes=[pltpu.SemaphoreType.DMA((3, pieces))],
-    )(*grads))
+        compiler_params=pltpu.CompilerParams(vmem_limit_bytes=16 * 1024 * 1024),
+    )(*[pltpu.with_memory_space_constraint(grad, pltpu.VMEM) for grad in grads]))
 
 
 def body(n_outer, n_inner, queries, key_rows, values, out_grads, offsets):
     tokens, columns = queries.shape
     rows = tokens // R_MID
     slots = -(-H_MID // n_inner)
-    anywhere = pl.BlockSpec(memory_space=pl.ANY)
     dma = pltpu.SemaphoreType.DMA
     grads = pl.pallas_call(
         functools.partial(kernel, n_outer, n_inner),
         out_shape=[jax.ShapeDtypeStruct((tokens, columns), BF16)] * 3,
         in_specs=[pl.BlockSpec(memory_space=pltpu.HBM)] * 5,
-        out_specs=[anywhere] * 3,
+        out_specs=[pl.BlockSpec(memory_space=pltpu.VMEM)] * 3,
         scratch_shapes=[
             pltpu.SMEM(offsets.shape, jnp.int32),
             pltpu.VMEM((4, tokens, columns), BF16),
-            pltpu.VMEM((3, tokens, columns), BF16),
             pltpu.VMEM((H_MID, 4, rows, HEAD_DIM), BF16),
             pltpu.VMEM((slots, n_inner, 4, rows, HEAD_DIM), BF16),
             pltpu.VMEM((slots, n_inner, 3, rows, HEAD_DIM), BF16),
@@ -368,11 +350,10 @@
             pltpu.VMEM((3, n_outer * n_inner * WIDE_ROWS, HEAD_DIM), F32),
             dma,
             dma((H_MID + 2, 4)),
-            dma((H_MID + 2, 3)),
             dma((H_MID,)),
             dma((slots, n_inner)),
-            dma((slots, n_inner)),
-            dma((H_MID,)),
+            dma((slots, n_inner, 3)),
+            dma((H_MID, 3)),
             dma((n_inner,)),
             dma((n_inner,)),
             dma((n_outer,)),

time: 98.6 us -> 25.9 us (0.26)
  Pallas kernels: 95.2 us -> 25.1 us
  local copies, waits for them, and re-layouts: 2.67 us -> 0 us
    pallas_call x1, Pallas kernels: 72.7 us -> 1.49 us  [write_out(): pl.pallas_call(copies, out_shape=[jax.ShapeDtypeStruct(grad.shape, grad.d...]
    unnamed x6 -> x0, local copies, waits for them, and re-layouts: 2.67 us -> none
    pallas_call x1, Pallas kernels: 22.5 us -> 23.6 us  [body(): pl.pallas_call(functools.partial(kernel, n_outer, n_inner), out_shape=[ja...]
where the time goes in v3:
time: 25.9 us; the launch traced here: 25.7 us
  Pallas kernels  25.1 us (97%)
  between operations  0.64 us (2%)
    pallas_call x1, Pallas kernels, body(): pl.pallas_call(functools.partial(kernel, n_outer, n_inner), out_shape=[ja...  23.6 us
    pallas_call x1, Pallas kernels, write_out(): pl.pallas_call(copies, out_shape=[jax.ShapeDtypeStruct(grad.shape, grad.d...  1.49 us

profile of v3, /device:TPU:0, one launch (start us, length us, event | category | flops | bytes accessed | tf_op | source)
XLA Modules:
  0.0 25.7 jit_solution(10156289760897958695)
XLA Ops:
  0.6 23.6 %shard_map.76 = (bf16[256,1536]{1,0:T(8,128)(2,1)S(1)}, bf16[256,1536]{1,0:T(8,128)(2,1)S(1)}, bf16[256,1536]{1,0:T(8,128)(2,1)S(1)}) custom-call(s32[8]{0:T(128)} %offsets_in.1, bf16[256,1536]{1,0:T(8,128)(2,1)} %queries.1, bf16[256,1536]{1,0:T(8,128)(2,1)} %key_rows.1, bf16[256,1536]{1,0:T(8,128)(2,1)} %values.1, bf16[256,1536]{1,0:T(8,128)(2,1)} %out_grads.1), custom_call_target="tpu_custom_call" | custom-call | tf_op jit(solution)/shard_map/pallas_call | solution.py:337
  24.3 1.5 %shard_map.77 = (bf16[256,1536]{1,0:T(8,128)(2,1)}, bf16[256,1536]{1,0:T(8,128)(2,1)}, bf16[256,1536]{1,0:T(8,128)(2,1)}) custom-call(bf16[256,1536]{1,0:T(8,128)(2,1)S(1)} %get-tuple-element.6.refs_0_, bf16[256,1536]{1,0:T(8,128)(2,1)S(1)} %get-tuple-element.7.refs_1_, bf16[256,1536]{1,0:T(8,128)(2,1)S(1)} %get-tuple-element.8.refs_2_), custom_call_target="tpu_custom_call" | custom-call | tf_op jit(solution)/shard_map/pallas_call | solution.py:322

commit v4 on v3

--- a/solution.py
+++ b/solution.py
@@ -29,13 +29,13 @@
 
 def attention_parts(q, k, v, g, mask=None):
     scale = 1.0 / math.sqrt(HEAD_DIM)
-    scores = dot(q, k, (1, 1)) * scale
+    scores = dot(k, q, (1, 1)) * scale
     if mask is not None:
         scores = jnp.where(mask, scores, -1e30)
-    exponent = jnp.exp(scores - jnp.max(scores, axis=1, keepdims=True))
-    weights = exponent * (1.0 / jnp.sum(exponent, axis=1, keepdims=True))
-    dots = dot(g, v, (1, 1))
-    row_dots = jnp.sum(weights * dots, axis=1, keepdims=True)
+    exponent = jnp.exp(scores - jnp.max(scores, axis=0, keepdims=True))
+    weights = exponent * (1.0 / jnp.sum(exponent, axis=0, keepdims=True))
+    dots = dot(v, g, (1, 1))
+    row_dots = jnp.sum(weights * dots, axis=0, keepdims=True)
     score_grads = (weights * (dots - row_dots) * scale).astype(BF16)
     return weights.astype(BF16), score_grads
 
@@ -174,12 +174,51 @@
         columns = slice(head * HEAD_DIM, (head + 1) * HEAD_DIM)
         q, k, v, g = [x[a, :, columns] for a in range(4)]
         weights, score_grads = attention_parts(q, k, v, g)
-        outputs[0][:, columns] = dot(score_grads, k, (1, 0)).astype(BF16)
-        outputs[1][:, columns] = dot(score_grads, q, (0, 0)).astype(BF16)
-        outputs[2][:, columns] = dot(weights, g, (0, 0)).astype(BF16)
-
-    for head in range(H_NEAR // 2):
-        near_head(head)
+        outputs[0][:, columns] = dot(score_grads, k, (0, 0)).astype(BF16)
+        outputs[1][:, columns] = dot(score_grads, q, (1, 0)).astype(BF16)
+        outputs[2][:, columns] = dot(weights, g, (1, 0)).astype(BF16)
+
+    def back_copy(slot, head, source, which):
+        return pltpu.make_async_remote_copy(
+            src_ref=result.at[slot, source, which], dst_ref=returned.at[head, which],
+            send_sem=back_send.at[slot, source, which], recv_sem=back_recv.at[head, which],
+            device_id=(me_o, source), device_id_type=MESH,
+        )
+
+    def owned(slot):
+        if slot == 0:
+            return me_i
+        shift = lax.rem(me_i + 2 * n_inner - n_inner // 2 + lax.rem(me_o, 2), n_inner)
+        return slot * n_inner + shift
+
+    segment = n_inner * rows
+    def own_slot(slot):
+        head = owned(slot)
+
+        @pl.when(head < H_MID)
+        def _():
+            for step in range(1, n_inner):
+                source = inner_peer(step)
+                mid_copy(0, slot, source, source).wait_recv()
+            q, k, v, g = [arrived[slot, :, a].reshape(segment, HEAD_DIM) for a in range(4)]
+            weights, score_grads = attention_parts(q, k, v, g)
+            for which, left, right, contract in (
+                (2, weights, g, (1, 0)), (1, score_grads, q, (1, 0)), (0, score_grads, k, (0, 0))
+            ):
+                grads = dot(left, right, contract).astype(BF16)
+                result[slot, :, which] = grads.reshape(n_inner, rows, HEAD_DIM)
+                for step in range(1, n_inner):
+                    back_copy(slot, head, inner_peer(step), which).start()
+                returned[head, which] = result[slot, me_i, which]
+
+    def first_near():
+        for head in range(H_NEAR // 2):
+            near_head(head)
+
+    several = owned(slots - 1) < H_MID if slots > 1 else me_i < 0
+    pl.when(jnp.logical_not(several))(first_near)
+    for slot in reversed(range(1, slots)):
+        own_slot(slot)
 
     for step in range(1, n_inner):
         line_copy(step, inner_peer(step)).wait_recv()
@@ -194,39 +233,8 @@
     for step in range(1, n_outer):
         plane_copy(step, me_o).start()
 
-    def back_copy(slot, head, source, which):
-        return pltpu.make_async_remote_copy(
-            src_ref=result.at[slot, source, which], dst_ref=returned.at[head, which],
-            send_sem=back_send.at[slot, source, which], recv_sem=back_recv.at[head, which],
-            device_id=(me_o, source), device_id_type=MESH,
-        )
-
-    def owned(slot):
-        if slot == 0:
-            return me_i
-        shift = lax.rem(me_i + 2 * n_inner - n_inner // 2 + lax.rem(me_o, 2), n_inner)
-        return slot * n_inner + shift
-
-    segment = n_inner * rows
-    for slot in reversed(range(slots)):
-        head = owned(slot)
-
-        @pl.when(head < H_MID)
-        def _():
-            for step in range(1, n_inner):
-                source = inner_peer(step)
-                mid_copy(0, slot, source, source).wait_recv()
-            q, k, v, g = [arrived[slot, :, a].reshape(segment, HEAD_DIM) for a in range(4)]
-            weights, score_grads = attention_parts(q, k, v, g)
-            for which, left, right, contract in (
-                (2, weights, g, (0, 0)), (0, score_grads, k, (1, 0)), (1, score_grads, q, (0, 0))
-            ):
-                grads = dot(left, right, contract).astype(BF16)
-                result[slot, :, which] = grads.reshape(n_inner, rows, HEAD_DIM)
-                for step in range(1, n_inner):
-                    back_copy(slot, head, inner_peer(step), which).start()
-                returned[head, which] = result[slot, me_i, which]
-
+    own_slot(0)
+    pl.when(several)(first_near)
     for head in range(H_NEAR // 2, H_NEAR):
         near_head(head)
 
@@ -246,12 +254,12 @@
     for first in range(0, total, tile):
         q = gathered(0, first // WIDE_ROWS, tile // WIDE_ROWS)
         g = gathered(3, first // WIDE_ROWS, tile // WIDE_ROWS)
-        query_head = lax.rem(lax.broadcasted_iota(jnp.int32, (tile, total), 0), WIDE_ROWS) // wide_tokens
-        key_head = lax.rem(lax.broadcasted_iota(jnp.int32, (tile, total), 1), WIDE_ROWS) // wide_tokens
-        weights, score_grads = attention_parts(q, wide_k, wide_v, g, query_head == key_head)
-        wide_result[0, first:first + tile] = dot(score_grads, wide_k, (1, 0))
-        wide_result[1] += dot(score_grads, q, (0, 0))
-        wide_result[2] += dot(weights, g, (0, 0))
+        key_head = lax.rem(lax.broadcasted_iota(jnp.int32, (total, 1), 0), WIDE_ROWS) // wide_tokens
+        query_head = lax.rem(lax.broadcasted_iota(jnp.int32, (1, tile), 1), WIDE_ROWS) // wide_tokens
+        weights, score_grads = attention_parts(q, wide_k, wide_v, g, key_head == query_head)
+        wide_result[0, first:first + tile] = dot(score_grads, wide_k, (0, 0))
+        wide_result[1] += dot(score_grads, q, (1, 0))
+        wide_result[2] += dot(weights, g, (1, 0))
     mine = pl.ds(pl.multiple_of((me_o * n_inner + me_i) * WIDE_ROWS, WIDE_ROWS), WIDE_ROWS)
     place = lax.broadcasted_iota(jnp.int32, (tokens, HEAD_DIM), 0)
     for which in range(3):
@@ -268,11 +276,12 @@
 
     spread_row = lax.broadcasted_iota(jnp.int32, (tokens, rows), 1)
     spread_position = lax.broadcasted_iota(jnp.int32, (tokens, rows), 0)
-    for head in range(H_MID):
+    returning = [lax.rem(me_i + step, H_MID - 1) for step in (0, 1, 3, 2)]
+    for head in (returning[0], jnp.int32(H_MID - 1), *returning[1:]):
         target = owner(head)
         place = (spread_position == spread_row * R_MID + offsets[head]).astype(F32).astype(BF16)
-        columns = slice(NEAR_END + head * HEAD_DIM, NEAR_END + (head + 1) * HEAD_DIM)
-        for which in (2, 0, 1):
+        columns = head_columns(head)
+        for which in (2, 1, 0):
 
             @pl.when(me_i != target)
             def _():

time: 25.9 us -> 25.1 us (0.969)
  Pallas kernels: 25.1 us -> 24.3 us
    pallas_call x1, Pallas kernels: 23.6 us -> 22.8 us  [body(): pl.pallas_call(functools.partial(kernel, n_outer, n_inner), out_shape=[ja...]
where the time goes in v4:
time: 25.1 us; the launch traced here: 24.9 us
  Pallas kernels  24.3 us (97%)
  between operations  0.64 us (3%)
    pallas_call x1, Pallas kernels, body(): pl.pallas_call(functools.partial(kernel, n_outer, n_inner), out_shape=[ja...  22.8 us
    pallas_call x1, Pallas kernels, write_out(): pl.pallas_call(copies, out_shape=[jax.ShapeDtypeStruct(grad.shape, grad.d...  1.49 us

profile of v4, /device:TPU:0, one launch (start us, length us, event | category | flops | bytes accessed | tf_op | source)
XLA Modules:
  0.0 24.9 jit_solution(12992166157718624540)
XLA Ops:
  0.6 22.8 %shard_map.76 = (bf16[256,1536]{1,0:T(8,128)(2,1)S(1)}, bf16[256,1536]{1,0:T(8,128)(2,1)S(1)}, bf16[256,1536]{1,0:T(8,128)(2,1)S(1)}) custom-call(s32[8]{0:T(128)} %offsets_in.1, bf16[256,1536]{1,0:T(8,128)(2,1)} %queries.1, bf16[256,1536]{1,0:T(8,128)(2,1)} %key_rows.1, bf16[256,1536]{1,0:T(8,128)(2,1)} %values.1, bf16[256,1536]{1,0:T(8,128)(2,1)} %out_grads.1), custom_call_target="tpu_custom_call" | custom-call | tf_op jit(solution)/shard_map/pallas_call | solution.py:346
  23.4 1.5 %shard_map.77 = (bf16[256,1536]{1,0:T(8,128)(2,1)}, bf16[256,1536]{1,0:T(8,128)(2,1)}, bf16[256,1536]{1,0:T(8,128)(2,1)}) custom-call(bf16[256,1536]{1,0:T(8,128)(2,1)S(1)} %get-tuple-element.6.refs_0_, bf16[256,1536]{1,0:T(8,128)(2,1)S(1)} %get-tuple-element.7.refs_1_, bf16[256,1536]{1,0:T(8,128)(2,1)S(1)} %get-tuple-element.8.refs_2_), custom_call_target="tpu_custom_call" | custom-call | tf_op jit(solution)/shard_map/pallas_call | solution.py:331

commit v5 on v4

--- a/solution.py
+++ b/solution.py
@@ -66,12 +66,15 @@
     for step in range(1, n_outer):
         pl.semaphore_signal(barrier, inc=1, device_id=(outer_peer(step), me_i), device_id_type=MESH)
 
-    first_head = jnp.where(me_i < n_inner // 2, (H_MID - 1) // 2, 0)
+    left = me_i < n_inner // 2
+    half = (H_MID - 1) // 2
 
     def head_at(step):
         if step == 0:
             return jnp.int32(H_MID - 1)
-        return lax.rem(first_head + step - 1, H_MID - 1)
+        return jnp.where(
+            left, lax.rem(half + step - 1, H_MID - 1), lax.rem(half + H_MID - 1 - step, H_MID - 1)
+        )
 
     def head_columns(head):
         return pl.ds(pl.multiple_of(NEAR_END + head * HEAD_DIM, HEAD_DIM), HEAD_DIM)
@@ -87,7 +90,7 @@
     offsets_load.start()
     loads = [load(step, head_columns(head_at(step))) for step in range(H_MID)]
     loads += [load(H_MID, wide_span), load(H_MID + 1, near_span)]
-    for group in (0, 1, H_MID, *range(2, H_MID), H_MID + 1):
+    for group in range(H_MID + 2):
         for copy in loads[group]:
             copy.start()
 
@@ -131,6 +134,10 @@
     send_head(0)
     pick_head(1)
     send_head(1)
+
+    for step in range(2, H_MID):
+        pick_head(step)
+        send_head(step)
 
     for copy in loads[H_MID]:
         copy.wait()
@@ -163,10 +170,6 @@
     for step in range(1, n_inner):
         line_copy(step, me_i).start()
 
-    for step in range(2, H_MID):
-        pick_head(step)
-        send_head(step)
-
     for copy in loads[H_MID + 1]:
         copy.wait()
 
@@ -191,7 +194,11 @@
         shift = lax.rem(me_i + 2 * n_inner - n_inner // 2 + lax.rem(me_o, 2), n_inner)
         return slot * n_inner + shift
 
+    def back_peer(step):
+        return inner_peer(jnp.where(lax.rem(me_i, 2) == 0, step, n_inner - step))
+
     segment = n_inner * rows
+
     def own_slot(slot):
         head = owned(slot)
 
@@ -207,8 +214,8 @@
             ):
                 grads = dot(left, right, contract).astype(BF16)
                 result[slot, :, which] = grads.reshape(n_inner, rows, HEAD_DIM)
-                for step in range(1, n_inner):
-                    back_copy(slot, head, inner_peer(step), which).start()
+                for step in (*range(n_inner // 2, n_inner), *range(1, n_inner // 2)):
+                    back_copy(slot, head, back_peer(step), which).start()
                 returned[head, which] = result[slot, me_i, which]
 
     def first_near():
@@ -219,6 +226,8 @@
     pl.when(jnp.logical_not(several))(first_near)
     for slot in reversed(range(1, slots)):
         own_slot(slot)
+
+    own_slot(0)
 
     for step in range(1, n_inner):
         line_copy(step, inner_peer(step)).wait_recv()
@@ -233,7 +242,6 @@
     for step in range(1, n_outer):
         plane_copy(step, me_o).start()
 
-    own_slot(0)
     pl.when(several)(first_near)
     for head in range(H_NEAR // 2, H_NEAR):
         near_head(head)

time: 25.1 us -> 26.2 us (1.044)
  Pallas kernels: 24.3 us -> 25.4 us
    pallas_call x1, Pallas kernels: 22.8 us -> 23.9 us  [body(): pl.pallas_call(functools.partial(kernel, n_outer, n_inner), out_shape=[ja...]
where the time goes in v5:
time: 26.2 us; the launch traced here: 26 us
  Pallas kernels  25.4 us (97%)
  between operations  0.64 us (2%)
    pallas_call x1, Pallas kernels, body(): pl.pallas_call(functools.partial(kernel, n_outer, n_inner), out_shape=[ja...  23.9 us
    pallas_call x1, Pallas kernels, write_out(): pl.pallas_call(copies, out_shape=[jax.ShapeDtypeStruct(grad.shape, grad.d...  1.49 us

profile of v5, /device:TPU:0, one launch (start us, length us, event | category | flops | bytes accessed | tf_op | source)
XLA Modules:
  0.0 26.0 jit_solution(825101141281242418)
XLA Ops:
  0.6 23.9 %shard_map.76 = (bf16[256,1536]{1,0:T(8,128)(2,1)S(1)}, bf16[256,1536]{1,0:T(8,128)(2,1)S(1)}, bf16[256,1536]{1,0:T(8,128)(2,1)S(1)}) custom-call(s32[8]{0:T(128)} %offsets_in.1, bf16[256,1536]{1,0:T(8,128)(2,1)} %queries.1, bf16[256,1536]{1,0:T(8,128)(2,1)} %key_rows.1, bf16[256,1536]{1,0:T(8,128)(2,1)} %values.1, bf16[256,1536]{1,0:T(8,128)(2,1)} %out_grads.1), custom_call_target="tpu_custom_call" | custom-call | tf_op jit(solution)/shard_map/pallas_call | solution.py:354
  24.5 1.5 %shard_map.77 = (bf16[256,1536]{1,0:T(8,128)(2,1)}, bf16[256,1536]{1,0:T(8,128)(2,1)}, bf16[256,1536]{1,0:T(8,128)(2,1)}) custom-call(bf16[256,1536]{1,0:T(8,128)(2,1)S(1)} %get-tuple-element.6.refs_0_, bf16[256,1536]{1,0:T(8,128)(2,1)S(1)} %get-tuple-element.7.refs_1_, bf16[256,1536]{1,0:T(8,128)(2,1)S(1)} %get-tuple-element.8.refs_2_), custom_call_target="tpu_custom_call" | custom-call | tf_op jit(solution)/shard_map/pallas_call | solution.py:339

commit v6 on v4

--- a/solution.py
+++ b/solution.py
@@ -66,12 +66,15 @@
     for step in range(1, n_outer):
         pl.semaphore_signal(barrier, inc=1, device_id=(outer_peer(step), me_i), device_id_type=MESH)
 
-    first_head = jnp.where(me_i < n_inner // 2, (H_MID - 1) // 2, 0)
+    left = me_i < n_inner // 2
+    half = (H_MID - 1) // 2
 
     def head_at(step):
         if step == 0:
             return jnp.int32(H_MID - 1)
-        return lax.rem(first_head + step - 1, H_MID - 1)
+        return jnp.where(
+            left, lax.rem(half + step - 1, H_MID - 1), lax.rem(half + H_MID - 1 - step, H_MID - 1)
+        )
 
     def head_columns(head):
         return pl.ds(pl.multiple_of(NEAR_END + head * HEAD_DIM, HEAD_DIM), HEAD_DIM)
@@ -178,10 +181,10 @@
         outputs[1][:, columns] = dot(score_grads, q, (1, 0)).astype(BF16)
         outputs[2][:, columns] = dot(weights, g, (1, 0)).astype(BF16)
 
-    def back_copy(slot, head, source, which):
+    def back_copy(slot, head, source):
         return pltpu.make_async_remote_copy(
-            src_ref=result.at[slot, source, which], dst_ref=returned.at[head, which],
-            send_sem=back_send.at[slot, source, which], recv_sem=back_recv.at[head, which],
+            src_ref=result.at[slot, source], dst_ref=returned.at[head],
+            send_sem=back_send.at[slot, source], recv_sem=back_recv.at[head],
             device_id=(me_o, source), device_id_type=MESH,
         )
 
@@ -191,7 +194,11 @@
         shift = lax.rem(me_i + 2 * n_inner - n_inner // 2 + lax.rem(me_o, 2), n_inner)
         return slot * n_inner + shift
 
+    def back_peer(step):
+        return inner_peer(jnp.where(lax.rem(me_i, 2) == 0, step, n_inner - step))
+
     segment = n_inner * rows
+
     def own_slot(slot):
         head = owned(slot)
 
@@ -207,13 +214,16 @@
             ):
                 grads = dot(left, right, contract).astype(BF16)
                 result[slot, :, which] = grads.reshape(n_inner, rows, HEAD_DIM)
-                for step in range(1, n_inner):
-                    back_copy(slot, head, inner_peer(step), which).start()
-                returned[head, which] = result[slot, me_i, which]
-
-    def first_near():
-        for head in range(H_NEAR // 2):
+            for step in (*range(n_inner // 2, n_inner), *range(1, n_inner // 2)):
+                back_copy(slot, head, back_peer(step)).start()
+            returned[head] = result[slot, me_i]
+
+    def near_heads(*heads):
+        for head in heads:
             near_head(head)
+
+    first_near = functools.partial(near_heads, *range(H_NEAR // 2))
+    second_near = functools.partial(near_heads, *range(H_NEAR // 2, H_NEAR))
 
     several = owned(slots - 1) < H_MID if slots > 1 else me_i < 0
     pl.when(jnp.logical_not(several))(first_near)
@@ -233,10 +243,9 @@
     for step in range(1, n_outer):
         plane_copy(step, me_o).start()
 
+    pl.when(jnp.logical_not(several))(second_near)
     own_slot(0)
-    pl.when(several)(first_near)
-    for head in range(H_NEAR // 2, H_NEAR):
-        near_head(head)
+    pl.when(several)(functools.partial(near_heads, *range(H_NEAR)))
 
     for step in range(1, n_outer):
         plane_copy(step, outer_peer(step)).wait_recv()
@@ -277,17 +286,20 @@
     spread_row = lax.broadcasted_iota(jnp.int32, (tokens, rows), 1)
     spread_position = lax.broadcasted_iota(jnp.int32, (tokens, rows), 0)
     returning = [lax.rem(me_i + step, H_MID - 1) for step in (0, 1, 3, 2)]
-    for head in (returning[0], jnp.int32(H_MID - 1), *returning[1:]):
-        target = owner(head)
-        place = (spread_position == spread_row * R_MID + offsets[head]).astype(F32).astype(BF16)
-        columns = head_columns(head)
-        for which in (2, 1, 0):
+    for group in ((returning[0], jnp.int32(H_MID - 1), returning[1]), returning[2:]):
+        for head in group:
+            target = owner(head)
 
             @pl.when(me_i != target)
             def _():
-                back_copy(0, head, target, which).wait_recv()
-
-            outputs[which][:, columns] = dot(place, returned[head, which], (1, 0)).astype(BF16)
+                back_copy(0, head, target).wait_recv()
+
+        for head in group:
+            place = (spread_position == spread_row * R_MID + offsets[head]).astype(F32).astype(BF16)
+            for which in range(3):
+                outputs[which][:, head_columns(head)] = dot(
+                    place, returned[head, which], (1, 0)
+                ).astype(BF16)
 
     for step in range(1, n_inner):
         line_copy(step, me_i).wait_send()
@@ -306,8 +318,7 @@
         @pl.when(head < H_MID)
         def _():
             for step in range(1, n_inner):
-                for which in range(3):
-                    back_copy(slot, head, inner_peer(step), which).wait_send()
+                back_copy(slot, head, inner_peer(step)).wait_send()
 
 
 def write_out(grads):
@@ -361,8 +372,8 @@
             dma((H_MID + 2, 4)),
             dma((H_MID,)),
             dma((slots, n_inner)),
-            dma((slots, n_inner, 3)),
-            dma((H_MID, 3)),
+            dma((slots, n_inner)),
+            dma((H_MID,)),
             dma((n_inner,)),
             dma((n_inner,)),
             dma((n_outer,)),

time: 25.1 us -> 24.4 us (0.972)
  Pallas kernels: 24.3 us -> 23.6 us
    pallas_call x1, Pallas kernels: 22.8 us -> 22.1 us  [body(): pl.pallas_call(functools.partial(kernel, n_outer, n_inner), out_shape=[ja...]
where the time goes in v6:
time: 24.4 us; the launch traced here: 24.3 us
  Pallas kernels  23.6 us (97%)
  between operations  0.64 us (3%)
    pallas_call x1, Pallas kernels, body(): pl.pallas_call(functools.partial(kernel, n_outer, n_inner), out_shape=[ja...  22.1 us
    pallas_call x1, Pallas kernels, write_out(): pl.pallas_call(copies, out_shape=[jax.ShapeDtypeStruct(grad.shape, grad.d...  1.49 us

profile of v6, /device:TPU:0, one launch (start us, length us, event | category | flops | bytes accessed | tf_op | source)
XLA Modules:
  0.0 24.3 jit_solution(17280864361932689729)
XLA Ops:
  0.6 22.1 %shard_map.76 = (bf16[256,1536]{1,0:T(8,128)(2,1)S(1)}, bf16[256,1536]{1,0:T(8,128)(2,1)S(1)}, bf16[256,1536]{1,0:T(8,128)(2,1)S(1)}) custom-call(s32[8]{0:T(128)} %offsets_in.1, bf16[256,1536]{1,0:T(8,128)(2,1)} %queries.1, bf16[256,1536]{1,0:T(8,128)(2,1)} %key_rows.1, bf16[256,1536]{1,0:T(8,128)(2,1)} %values.1, bf16[256,1536]{1,0:T(8,128)(2,1)} %out_grads.1), custom_call_target="tpu_custom_call" | custom-call | tf_op jit(solution)/shard_map/pallas_call | solution.py:357
  22.8 1.5 %shard_map.77 = (bf16[256,1536]{1,0:T(8,128)(2,1)}, bf16[256,1536]{1,0:T(8,128)(2,1)}, bf16[256,1536]{1,0:T(8,128)(2,1)}) custom-call(bf16[256,1536]{1,0:T(8,128)(2,1)S(1)} %get-tuple-element.6.refs_0_, bf16[256,1536]{1,0:T(8,128)(2,1)S(1)} %get-tuple-element.7.refs_1_, bf16[256,1536]{1,0:T(8,128)(2,1)S(1)} %get-tuple-element.8.refs_2_), custom_call_target="tpu_custom_call" | custom-call | tf_op jit(solution)/shard_map/pallas_call | solution.py:342
